TPU v7x, 32 devices: a whole 2x2x4 slice. The times are simulated.
32 devices in a mesh: cyl: 2 (over y), chain: 4 (over z), tensor: 4 (over x, core).
Axes of the slice: x: 2, y: 2, z: 4, core: 2. Of those that a mesh axis runs over, the one named last changes fastest.
Arguments:
- env: bfloat16 [8, 32, 10, 128, 128], P(('cyl', 'chain'), 'tensor'), parts along dimension 0, may hold values from -8 to 8, as said below
- site: bfloat16 [8, 32, 128, 128], P(('cyl', 'chain'), 'tensor'), parts along dimension 0, may hold values from -0.5 to 0.5
- seg_weight: float32 [8, 32, 128], P(('cyl', 'chain'), 'tensor'), parts along dimension 0, may hold values from 0.7 to 1.4
- ranks: int32 [64], P(('cyl', 'tensor')), parts along dimension 0, may hold values from 32 to 128
- mpo_mask: int32 [64, 10], P(('cyl', 'tensor')), parts along dimension 0, may hold values 0 or 1
Outputs:
- psi: bfloat16 [8, 32, 128, 128], P(('cyl', 'chain'), 'tensor'), parts along dimension 0
- energy: float32 [8], P(('cyl', 'chain')), parts along dimension 0
There are 2 independent parts, one for each index of `cyl`. A program takes and returns all parts, laid end to end along the dimension named above; each array names one. Nothing has to cross between parts.
Inputs may be any that keep to these rules, and one draw needn't show every extreme that they name: `env`: every environment block is symmetric in its last two dimensions.
All inputs are finite; a program needn't handle non-finite values. No bound on the sum of `mpo_mask` on one device may be relied on, other than what follows from the above.
Results may differ from a plain program's by a relative error of at most 0.011.
Values may be sent and summed in bfloat16 or wider, within the bound.
No kernel may reach another device: no remote copies, remote signals or barrier semaphores. Data moves between devices by JAX's collectives and lax.ppermute only.
A program may use at most 192 MiB of HBM per device.

v0:
```python
import jax
import jax.numpy as jnp
from jax import lax
from jax.sharding import PartitionSpec as P

ITERS = 4


STEP_SIZE = 0.5


def carried_in(value, axis, join, neutral):
    count, mine = (lax.axis_size(axis), lax.axis_index(axis))
    pieces = lax.all_gather(value, axis)
    so_far = jnp.full_like(value, 0) + jnp.asarray(neutral, value.dtype)

    def turn(position, so_far):
        longer = join(so_far, pieces[position])
        return jnp.where(position < mine, longer, so_far)

    return lax.fori_loop(0, count - 1, turn, so_far)


def from_partner(value, axis, distance):
    mask = 2**distance
    pairs = [(source, source ^ mask) for source in range(lax.axis_size(axis))]
    return lax.ppermute(value, axis, pairs)


def solve_boundary(left, right, left_site, right_site, ranks, mpo_mask, count, totals):
    hi = lax.Precision.HIGHEST
    sectors = left.shape[0]
    chans = left.shape[1]
    edge = left.shape[2]
    rowmask = (jnp.arange(edge)[None, :] < ranks[:, None]).astype(jnp.float32)[:, :, None]
    weights = mpo_mask.astype(jnp.float32)
    start = jnp.einsum("sij,sjk->sik", left_site, right_site, preferred_element_type=jnp.float32)
    vector = rowmask * start
    diag_left = jnp.diagonal(left, axis1=2, axis2=3).astype(jnp.float32)
    diag_right = jnp.diagonal(right, axis1=2, axis2=3).astype(jnp.float32)
    diag_h = jnp.einsum("swi,swj->sij", weights[:, :, None] * diag_left, diag_right, precision=hi)
    mask_b = mpo_mask.astype(jnp.bfloat16)[:, :, None, None]
    left_flat = left.reshape(sectors, chans * edge, edge)
    theta = jnp.float32(0.0)
    for step in range(ITERS):
        low = vector.astype(jnp.bfloat16)
        inner = (
            jnp.einsum("sij,swjk->swik", low, right, preferred_element_type=jnp.float32).astype(
                jnp.bfloat16
            )
            * mask_b
        )
        inner_flat = inner.reshape(sectors, chans * edge, edge)
        image = rowmask * jnp.einsum(
            "sxi,sxk->sik", left_flat, inner_flat, preferred_element_type=jnp.float32
        )
        sums = totals(jnp.stack([jnp.sum(vector * image), jnp.sum(vector * vector)]))
        theta = sums[0] / (sums[1] + 1e-06)
        resid = image - theta * vector
        correct = resid / (1.0 + jnp.abs(diag_h - theta))
        vector = (vector - STEP_SIZE * correct) / jnp.sqrt(sums[1] / count + 1e-06)
    final = totals(jnp.stack([jnp.sum(vector * vector)]))
    return ((vector / jnp.sqrt(final[0] / count + 1e-06)).astype(jnp.bfloat16), theta)


def order_roles(is_left, own_env, other_env, own_site, other_site):
    return lax.cond(
        is_left,
        lambda: (own_env, other_env, own_site, other_site),
        lambda: (other_env, own_env, other_site, own_site),
    )


def local(env, site, seg_weight, ranks, mpo_mask):
    parity = lax.axis_index("chain") % 2
    is_left = parity == 0
    own_weight = seg_weight[0]
    before = carried_in(
        own_weight, "chain", lambda earlier, later: earlier * later, jnp.ones_like(own_weight)
    )
    scale = jnp.where(is_left, before * own_weight, own_weight)
    scaled = (scale[:, None, :, None] * env[0] * scale[:, None, None, :]).astype(jnp.bfloat16)
    mine_site = site[0]
    sectors = scaled.shape[0]
    edge = scaled.shape[2]
    count = float(sectors * lax.axis_size("tensor") * edge * edge)
    partner_env, partner_site = from_partner((scaled, mine_site), "chain", 0)

    def totals(values):
        return lax.psum(values, "tensor")

    left, right, left_site, right_site = order_roles(
        is_left, scaled, partner_env, mine_site, partner_site
    )
    psi, theta = solve_boundary(left, right, left_site, right_site, ranks, mpo_mask, count, totals)
    return (psi[None], jnp.reshape(theta, (1,)))


def solution(mesh):
    in_specs = (
        P(("cyl", "chain"), "tensor", None, None, None),
        P(("cyl", "chain"), "tensor", None, None),
        P(("cyl", "chain"), "tensor", None),
        P(("cyl", "tensor")),
        P(("cyl", "tensor"), None),
    )
    out_specs = (P(("cyl", "chain"), "tensor", None, None), P(("cyl", "chain")))
    return jax.shard_map(local, mesh=mesh, in_specs=in_specs, out_specs=out_specs, check_vma=False)
```

profile of v0, /device:TPU:0, one launch (start us, length us, event | category | flops | bytes accessed | tf_op | source)
XLA Modules:
  0.0 207.6 jit_solution(9474877851227548535)
XLA Ops:
  0.6 1.0 copy.59
  1.6 14.9 %all_gather.3 = f32[4,8,128]{2,1,0:T(8,128)S(1)} all-gather(f32[1,8,128]{2,1,0:T(8,128)} %param.11), channel_id=1, replica_groups=mesh['cyl'=2,'chain'=4,'tensor'=4] {'chain'}, dimensions={0}, use_global_device_ids=true | all-gather | bytes 20480 | tf_op jit(solution)/shard_map/all_gather | solution.py:14
  16.5 0.1 while.14
  16.6 0.7 multiply_select_fusion.1
  17.3 0.0 copy-start.7
  17.3 0.0 copy-start.6
  17.3 2.7 %fusion.1 = bf16[8,10,128,128]{3,2,1,0:T(8,128)(2,1)S(1)} fusion(bf16[1,8,10,128,128]{4,3,2,1,0:T(8,128)(2,1)} %param.9, f32[8,128]{1,0:T(8,128)S(1)} %multiply_select_fusion.1), kind=kLoop, calls=%fused_computation.5 | loop fusion | flops 5242880 | bytes 5246976 | tf_op jit(solution)/shard_map/convert_element_type | solution.py:82
  20.0 1.6 collective-permute-start
  21.6 0.4 collective-permute-start.1
  22.1 0.0 copy-done.7
  22.1 0.1 fusion.14
  22.1 0.0 copy-done.6
  22.2 59.2 %collective-permute-done.1 = bf16[8,128,128]{2,1,0:T(8,128)(2,1)S(1)} collective-permute-done((bf16[8,128,128]{2,1,0:T(8,128)(2,1)S(1)}, bf16[8,128,128]{2,1,0:T(8,128)(2,1)S(1)}, u32[]{:S(2)}, u32[]{:S(2)}) %collective-permute-start.1) | collective-permute-done | bytes 262176 | tf_op jit(solution)/shard_map/ppermute | solution.py:27
  81.4 0.0 collective-permute-done
  81.4 4.8 %conditional.1 = (bf16[8,10,128,128]{3,2,1,0:T(8,128)(2,1)}, bf16[8,10,128,128]{3,2,1,0:T(8,128)(2,1)S(1)}, bf16[8,128,128]{2,1,0:T(8,128)(2,1)S(1)}, bf16[8,128...) conditional(s32[]{:T(128)} %convert_element_type.61, (bf16[8,10,128,128]{3,2,1,0:T(8,128)(2,1)}, ...), branch_computations={%region_2.3_spmd, %region_3.4_spmd} | conditional | bytes 16777256 | solution.py:67
  81.4 1.5 copy.54
  82.9 1.5 copy.58
  84.4 1.7 copy.55
  86.2 0.0 copy-start.4
  86.2 20.2 %copy.20 = bf16[8,10,128,128]{1,0,3,2:T(8,128)(2,1)} copy(bf16[8,10,128,128]{3,2,1,0:T(8,128)(2,1)} %get-tuple-element.164) | data formatting | bytes 5242880 | tf_op jit(solution)/shard_map/cond | solution.py:67
  106.4 0.0 copy-done.4
  106.4 19.7 %copy.21 = bf16[8,10,128,128]{1,0,3,2:T(8,128)(2,1)} copy(bf16[8,10,128,128]{3,2,1,0:T(8,128)(2,1)S(1)} %get-tuple-element.165) | data formatting | bytes 5242880 | tf_op jit(solution)/shard_map/cond | solution.py:67
  126.2 2.5 %gather_fusion = bf16[128,8,10]{2,1,0:T(8,128)(2,1)} fusion(bf16[8,10,128,128]{1,0,3,2:T(8,128)(2,1)} %copy.20, s32[128]{0:T(128)S(1)} %or_bitcast_fusion), kind=kCustom, calls=%fused_computation | custom fusion | bytes 41984 | tf_op jit(solution)/shard_map/jit(diagonal)/gather | solution.py:39
  128.7 1.2 convolution_multiply_fusion.4
  129.8 0.8 convert_multiply_fusion.4
  130.7 0.0 copy-start.5
  130.7 4.3 %multiply_reduce_fusion.8 = (f32[]{:T(128)}, f32[]{:T(128)}, f32[8,128,128]{2,1,0:T(8,128)}) fusion(f32[8,128,128]{2,1,0:T(8,128)S(1)} %convolution_multiply_fusion.4, bf16[8,1280,128]{2,1,0:T(8,128)(2,1)} %get-tuple-element.174, bf16[8,1280,128]{2,1,0:T(8,128)(2,1)S(1)} %bitcast.85, f32[8,128]{1,0:T(8,128)S(1)} %fusion.14), kind=kOutput, calls=%fused_computation.31 | convolution fusion | flops 336199680 | bytes 6295560 | tf_op jit(solution)/shard_map/sxi,sxk->sik/dot_general | solution.py:54
  135.0 1.4 pad_maximum_fusion
  136.3 2.5 %gather_fusion.1 = bf16[128,8,10]{2,1,0:T(8,128)(2,1)} fusion(bf16[8,10,128,128]{1,0,3,2:T(8,128)(2,1)} %copy.21, s32[128]{0:T(128)S(1)} %or_bitcast_fusion), kind=kCustom, calls=%fused_computation.1 | custom fusion | bytes 41984 | tf_op jit(solution)/shard_map/jit(diagonal)/gather | solution.py:40
  138.8 5.6 %psum.35 = f32[2]{0:T(128)S(1)} all-reduce(f32[2]{0:T(128)S(1)} %pad_maximum_fusion), channel_id=1, replica_groups=mesh['cyl'=2,'chain'=4,'tensor'=4] {'tensor'}, use_global_device_ids=true, to_apply=%region_6.7 | all-reduce | flops 2 | bytes 16 | tf_op jit(solution)/shard_map/psum | solution.py:90
  144.4 0.7 fusion.19
  146.5 0.0 copy-done.5
  147.2 2.7 %subtract_divide_fusion.2 = (f32[8,128,128]{2,1,0:T(8,128)S(1)}, f32[8,128,128]{2,1,0:T(8,128)}) fusion(f32[8,128,128]{2,1,0:T(8,128)S(1)} %convolution_multiply_fusion.4, f32[8,128,128]{2,1,0:T(8,128)} %get-tuple-element.218, f32[]{:T(128)} %bitcast.15, f32[]{:T(128)} %bitcast.11, bf16[8,10,128]{1,0,2:T(8,128)(2,1)} %bitcast.91, ...), kind=kOutput, calls=%fused_computation.29 | convolution fusion | flops 16908288 | bytes 2158600 | tf_op jit(solution)/shard_map/swi,swj->sij/dot_general | solution.py:41
  149.9 0.0 copy-start.3
  149.9 0.8 convert_multiply_fusion.3
  150.8 0.0 copy-done.3
  150.8 0.0 copy-start.1
  150.8 4.3 %multiply_reduce_fusion.6 = (f32[]{:T(128)}, f32[]{:T(128)}, f32[8,128,128]{2,1,0:T(8,128)}) fusion(f32[8,128,128]{2,1,0:T(8,128)S(1)} %get-tuple-element.219, bf16[8,1280,128]{2,1,0:T(8,128)(2,1)} %get-tuple-element.174, bf16[8,1280,128]{2,1,0:T(8,128)(2,1)S(1)} %bitcast.86, f32[8,128]{1,0:T(8,128)S(1)} %fusion.14), kind=kOutput, calls=%fused_computation.28 | convolution fusion | flops 336199680 | bytes 6295560 | tf_op jit(solution)/shard_map/sxi,sxk->sik/dot_general | solution.py:54
  155.1 1.4 pad_maximum_fusion.1
  156.4 6.6 %psum.36 = f32[2]{0:T(128)S(1)} all-reduce(f32[2]{0:T(128)S(1)} %pad_maximum_fusion.1), channel_id=1, replica_groups=mesh['cyl'=2,'chain'=4,'tensor'=4] {'tensor'}, use_global_device_ids=true, to_apply=%region_9.10 | all-reduce | flops 2 | bytes 16 | tf_op jit(solution)/shard_map/psum | solution.py:90
  163.0 0.6 fusion.18
  165.6 0.0 copy-done.1
  165.6 1.4 subtract_divide_fusion.1
  167.0 0.0 copy-start
  167.0 0.8 convert_multiply_fusion.2
  167.9 0.0 copy-done
  167.9 4.2 %multiply_reduce_fusion.4 = (f32[]{:T(128)}, f32[]{:T(128)}, f32[8,128,128]{2,1,0:T(8,128)}) fusion(f32[8,128,128]{2,1,0:T(8,128)S(1)} %subtract_divide_fusion.1, bf16[8,1280,128]{2,1,0:T(8,128)(2,1)} %get-tuple-element.174, bf16[8,1280,128]{2,1,0:T(8,128)(2,1)S(1)} %bitcast.87, f32[8,128]{1,0:T(8,128)S(1)} %fusion.14), kind=kOutput, calls=%fused_computation.25 | convolution fusion | flops 336199680 | bytes 6295560 | tf_op jit(solution)/shard_map/sxi,sxk->sik/dot_general | solution.py:54
  172.1 1.4 pad_maximum_fusion.2
  173.5 6.0 %psum.37 = f32[2]{0:T(128)S(1)} all-reduce(f32[2]{0:T(128)S(1)} %pad_maximum_fusion.2), channel_id=1, replica_groups=mesh['cyl'=2,'chain'=4,'tensor'=4] {'tensor'}, use_global_device_ids=true, to_apply=%region_12.13 | all-reduce | flops 2 | bytes 16 | tf_op jit(solution)/shard_map/psum | solution.py:90
  179.5 0.6 fusion.17
  182.1 1.5 subtract_divide_fusion
  183.6 0.8 convert_multiply_fusion.1
  184.5 0.0 copy-start.2
  184.5 3.5 %multiply_reduce_fusion.2 = (f32[]{:T(128)}, f32[]{:T(128)}, f32[8,128,128]{2,1,0:T(8,128)S(1)}) fusion(f32[8,128,128]{2,1,0:T(8,128)S(1)} %subtract_divide_fusion, bf16[8,1280,128]{2,1,0:T(8,128)(2,1)} %get-tuple-element.174, bf16[8,1280,128]{2,1,0:T(8,128)(2,1)S(1)} %bitcast.84, f32[8,128]{1,0:T(8,128)S(1)} %fusion.14), kind=kOutput, calls=%fused_computation.22 | convolution fusion | flops 336199680 | bytes 6295560 | tf_op jit(solution)/shard_map/sxi,sxk->sik/dot_general | solution.py:54
  188.0 1.4 pad_maximum_fusion.3
  189.3 6.0 %psum.38 = f32[2]{0:T(128)S(1)} all-reduce(f32[2]{0:T(128)S(1)} %pad_maximum_fusion.3), channel_id=1, replica_groups=mesh['cyl'=2,'chain'=4,'tensor'=4] {'tensor'}, use_global_device_ids=true, to_apply=%region_15.16 | all-reduce | flops 2 | bytes 16 | tf_op jit(solution)/shard_map/psum | solution.py:90
  195.3 0.6 fusion.16
  197.9 0.0 copy-done.2
  197.9 0.9 multiply_reduce_fusion
  198.8 6.3 %psum.39 = f32[1]{0:T(128)} all-reduce(f32[1]{0:T(128)} %bitcast.40), channel_id=1, replica_groups=mesh['cyl'=2,'chain'=4,'tensor'=4] {'tensor'}, use_global_device_ids=true, to_apply=%region_17.18 | all-reduce | flops 1 | bytes 8 | tf_op jit(solution)/shard_map/psum | solution.py:90
  205.7 0.8 fusion.13
  (9 shorter events, 0.1 us)
Async XLA Ops:
  17.3 4.8 %copy-start.7 = (s32[8]{0:T(128)S(1)}, s32[8]{0:T(128)}, u32[]{:S(2)}) copy-start(s32[8]{0:T(128)} %param.12) | copy-start | bytes 100
  17.3 4.8 %copy-start.6 = (s32[8,10]{1,0:T(8,128)S(1)}, s32[8,10]{1,0:T(8,128)}, u32[]{:S(2)}) copy-start(s32[8,10]{1,0:T(8,128)} %param.13) | copy-start | bytes 964
  20.0 61.4 %collective-permute-start = (bf16[8,10,128,128]{3,2,1,0:T(8,128)(2,1)S(1)}, bf16[8,10,128,128]{3,2,1,0:T(8,128)(2,1)}, u32[]{:S(2)}, u32[]{:S(2)}) collective-permute-start(bf16[8,10,128,128]{3,2,1,0:T(8,128)(2,1)S(1)} %fusion.1), channel_id=1, source_target_pairs={{0,4},{4,0},{8,12},{12,8},{1,5},{5,1},{9,13},{13,9},{2,6},{6,2},{1... | collective-permute-start | bytes 7864328 | tf_op jit(solution)/shard_map/ppermute | solution.py:27
  21.6 59.8 %collective-permute-start.1 = (bf16[8,128,128]{2,1,0:T(8,128)(2,1)S(1)}, bf16[8,128,128]{2,1,0:T(8,128)(2,1)S(1)}, u32[]{:S(2)}, u32[]{:S(2)}) collective-permute-start(bf16[8,128,128]{2,1,0:T(8,128)(2,1)S(1)} %bitcast.88), channel_id=1, source_target_pairs={{0,4},{4,0},{8,12},{12,8},{1,5},{5,1},{9,13},{13,9},{2,6},{6,2},{1... | collective-permute-start | bytes 786440 | tf_op jit(solution)/shard_map/ppermute | solution.py:27
  86.2 20.2 %copy-start.4 = (bf16[8,128,128]{2,1,0:T(8,128)(2,1)}, bf16[8,128,128]{2,1,0:T(8,128)(2,1)S(1)}, u32[]{:S(2)}) copy-start(bf16[8,128,128]{2,1,0:T(8,128)(2,1)S(1)} %get-tuple-element.162) | copy-start | bytes 786436
  130.7 15.8 %copy-start.5 = (bf16[128,8,10]{2,1,0:T(8,128)(2,1)S(1)}, bf16[128,8,10]{2,1,0:T(8,128)(2,1)}, u32[]{:S(2)}) copy-start(bf16[128,8,10]{2,1,0:T(8,128)(2,1)} %gather_fusion) | copy-start | bytes 61444
  149.9 0.8 copy-start.3
  150.8 14.8 %copy-start.1 = (f32[8,128,128]{2,1,0:T(8,128)S(1)}, f32[8,128,128]{2,1,0:T(8,128)}, u32[]{:S(2)}) copy-start(f32[8,128,128]{2,1,0:T(8,128)} %get-tuple-element.220) | copy-start | bytes 1572868
  167.0 0.9 copy-start
  184.5 13.4 %copy-start.2 = (f32[8,128,128]{2,1,0:T(8,128)S(1)}, f32[8,128,128]{2,1,0:T(8,128)}, u32[]{:S(2)}) copy-start(f32[8,128,128]{2,1,0:T(8,128)} %get-tuple-element.220) | copy-start | bytes 1572868
where the time goes:
time: 209 us; the launch traced here: 208 us
  waiting for transfers between devices  59.2 us (28%)
  local copies, waits for them, and re-layouts  53.1 us (25%)
  blocking collectives  45.4 us (22%)
  matrix products  23.5 us (11%)
  other arithmetic  13.5 us (6%)
  between operations  10.6 us (5%)
  starting transfers between devices  2.09 us (1%)
    ppermute x2, waiting for transfers between devices, from_partner(): return lax.ppermute(value, axis, pairs)  59.2 us
    cond x2, local copies, waits for them, and re-layouts, order_roles(): lax.cond(is_left, lambda: (own_env, other_env, own_site, other_site), lam...  39.9 us
    psum x5, blocking collectives, totals(): return lax.psum(values, 'tensor')  30.5 us
    dot_general x4, matrix products, solve_boundary(): jnp.einsum('sxi,sxk->sik', left_flat, inner_flat, preferred_element_type=...  16.2 us
    all_gather x1, blocking collectives, carried_in(): pieces = lax.all_gather(value, axis)  14.9 us
    another operation x4, other arithmetic, solve_boundary(): jnp.stack([jnp.sum(vector * image), jnp.sum(vector * vector)])  5.46 us
    cond x5, local copies, waits for them, and re-layouts  4.84 us
  transfers between devices with their start and end apart: 2, of which 1 were waited for; matrix products, arithmetic and copies ran while one was open for 0% of the time, Pallas kernels for 0%

commit v1 on v0

v1 whole, which is shorter than its diff:
```python
import functools

import jax
import jax.numpy as jnp
from jax import lax
from jax.experimental import pallas as pl
from jax.experimental.pallas import tpu as pltpu
from jax.sharding import PartitionSpec as P

ITERS = 4
STEP_SIZE = 0.5
EPS = 1e-6
BF16 = jnp.bfloat16
F32 = jnp.float32
VMEM_LIMIT = 48 * 2**20
VM = pl.BlockSpec(memory_space=pltpu.VMEM)
SM = pl.BlockSpec(memory_space=pltpu.SMEM)


def params():
    return pltpu.CompilerParams(vmem_limit_bytes=VMEM_LIMIT)


def cost(flops, bytes_accessed):
    return pl.CostEstimate(flops=int(flops), bytes_accessed=int(bytes_accessed), transcendentals=0)


def vmem(shape, dtype):
    return pltpu.VMEM(shape, dtype)


def keep(x):
    return pltpu.with_memory_space_constraint(x, pltpu.VMEM)


def grid_ij(edge):
    i = lax.broadcasted_iota(jnp.int32, (edge, edge), 0)
    j = lax.broadcasted_iota(jnp.int32, (edge, edge), 1)
    return i, j


def diag_row(block, i, j):
    return jnp.sum(jnp.where(i == j, block, 0.0), axis=0, keepdims=True)


def pack_kernel(cuts, sectors, chans, mask_ref, env_ref, *refs):
    chunks = refs[: len(cuts)]
    where_ref, diag_ref = refs[len(cuts) :]
    edge = env_ref.shape[-1]
    n = jnp.int32(0)
    for s in range(sectors):
        k = jnp.int32(0)
        for w in range(chans):
            m = mask_ref[s, w]
            where_ref[0, n] = jnp.int32(s * chans + w)
            where_ref[1, n] = jnp.int32(s)
            where_ref[2, n] = k
            n = n + m
            k = k + m
    where_ref[0, n] = jnp.int32(0)
    where_ref[1, n] = jnp.int32(0)
    where_ref[2, n] = jnp.int32(0)
    where_ref[3, 0] = n
    i, j = grid_ij(edge)
    pairs = (n + 1) // 2
    for (low, high), out in zip(cuts, chunks):

        def body(p, carry, low=low, out=out):
            first = env_ref[where_ref[0, 2 * p]].astype(F32)
            second = env_ref[where_ref[0, 2 * p + 1]].astype(F32)
            at = pl.multiple_of((p - low) * edge, edge)
            out[pl.ds(at, edge), :] = jnp.where(i <= j, first, second).astype(BF16)
            diag_ref[pl.ds(p - low, 1), :] = diag_row(second, i, j)
            return carry

        lax.fori_loop(low, jnp.minimum(high, pairs), body, 0)
        tail = out.shape[0] - (high - low) * edge
        out[(high - low) * edge :, :] = diag_ref[:tail, :].astype(BF16)


def unpack(low, high, here, chunk, where_ref, outer, buf, diags):
    edge = chunk.shape[-1]
    sectors = diags.shape[1]
    i, j = grid_ij(edge)
    n = where_ref[3, 0]

    def put(k, block):
        s, c = where_ref[1, k], where_ref[2, k]
        low_block = (block * outer[s]).astype(BF16)
        buf[here, s, c] = low_block
        diags[here, s, pl.ds(c, 1), :] = diag_row(low_block.astype(F32), i, j)

    tail = chunk[(high - low) * edge :, :].astype(F32)
    rows = lax.broadcasted_iota(jnp.int32, tail.shape, 0)

    def body(p, carry):
        at = pl.multiple_of((p - low) * edge, edge)
        both = chunk[pl.ds(at, edge), :].astype(F32)
        flip = both.T
        put(2 * p, jnp.where(i <= j, both, flip))

        @pl.when(2 * p + 1 < n)
        def _():
            diag = jnp.sum(jnp.where(rows == p - low, tail, 0.0), axis=0, keepdims=True)
            put(2 * p + 1, jnp.where(i > j, both, jnp.where(i == j, diag, flip)))

        return carry

    lax.fori_loop(low, jnp.minimum(high, (n + 1) // 2), body, 0)


def own_kernel(cut, where_ref, env_ref, weights, chunk, buf, diags, outer, mine):
    count, sectors, edge = weights.shape
    chans = buf.shape[2]
    at = lax.axis_index("chain")
    side = at % 2
    i, j = grid_ij(edge)
    left = weights[0]
    for c in range(1, count):
        left = left * jnp.where(c <= at - side, weights[c], 1.0)
    right = weights[at - side + 1]
    for s in range(sectors):
        row_l = jnp.broadcast_to(left[s : s + 1, :], (edge, edge))
        row_r = jnp.broadcast_to(right[s : s + 1, :], (edge, edge))
        outer_l = row_l.T * row_l
        outer_r = row_r.T * row_r
        mine[s] = jnp.where(side == 0, outer_l, outer_r)
        outer[s] = jnp.where(side == 0, outer_r, outer_l)
    diags[...] = jnp.zeros_like(diags)

    def wipe(t, carry):
        buf[0, t // chans, t % chans] = jnp.zeros((edge, edge), BF16)
        buf[1, t // chans, t % chans] = jnp.zeros((edge, edge), BF16)
        return carry

    lax.fori_loop(0, sectors * chans, wipe, 0)

    def body(k, carry):
        s, c = where_ref[1, k], where_ref[2, k]
        block = (env_ref[where_ref[0, k]].astype(F32) * mine[s]).astype(BF16)
        buf[side, s, c] = block
        diags[side, s, pl.ds(c, 1), :] = diag_row(block.astype(F32), i, j)
        return carry

    lax.fori_loop(0, where_ref[3, 0], body, 0)
    unpack(cut[0], cut[1], 1 - side, chunk, where_ref, outer, buf, diags)


def matvec(s, vector, buf, keep_row):
    chans = buf.shape[2]
    low = vector.astype(BF16)
    total = None
    for c in range(0, chans, 2):
        width = min(2, chans - c)
        right = jnp.concatenate([buf[1, s, c + d] for d in range(width)], axis=1)
        left = jnp.concatenate([buf[0, s, c + d] for d in range(width)], axis=1)
        edge = left.shape[0]
        inner = jnp.dot(low, right, preferred_element_type=F32).astype(BF16)
        inner = jnp.concatenate([inner[:, d * edge : (d + 1) * edge] for d in range(width)], axis=0)
        term = jnp.dot(left, inner, preferred_element_type=F32)
        total = term if total is None else total + term
    return jnp.where(keep_row, total, 0.0)


def store_sums(part, along, square):
    part[0:1, :] = jnp.sum(along, axis=0, keepdims=True)
    part[1:2, :] = jnp.sum(square, axis=0, keepdims=True)


def apply_all(vectors, ranks_ref, buf, vec, image, part):
    sectors, edge = buf.shape[1], buf.shape[-1]
    i, _ = grid_ij(edge)
    along = jnp.zeros((edge, edge), F32)
    square = jnp.zeros((edge, edge), F32)
    for s in range(sectors):
        vector = vectors(s)
        vec[s] = vector
        hv = matvec(s, vector, buf, i < ranks_ref[s])
        image[s] = hv
        along = along + vector * hv
        square = square + vector * vector
    store_sums(part, along, square)


def first_kernel(
    cuts, where_ref, ranks_ref, outer, own_site, other_site, *refs
):
    chunks = refs[: len(cuts)]
    _, _, buf, diags, vec, image, dh, part = refs[len(cuts) :]
    sectors, edge = buf.shape[1], buf.shape[-1]
    side = lax.axis_index("chain") % 2
    i, _ = grid_ij(edge)
    for (low, high), chunk in zip(cuts, chunks):
        unpack(low, high, 1 - side, chunk, where_ref, outer, buf, diags)

    def start(s):
        dh[s] = lax.dot_general(
            diags[0, s].astype(BF16),
            diags[1, s].astype(BF16),
            (((0,), (0,)), ((), ())),
            preferred_element_type=F32,
        )
        left = jnp.where(side == 0, own_site[s], other_site[s])
        right = jnp.where(side == 0, other_site[s], own_site[s])
        return jnp.where(i < ranks_ref[s], jnp.dot(left, right, preferred_element_type=F32), 0.0)

    apply_all(start, ranks_ref, buf, vec, image, part)


def joined(parts):
    values = [p[...] for p in parts]
    while len(values) > 1:
        values = [values[k] + values[k + 1] for k in range(0, len(values), 2)]
    total = values[0]
    along = jnp.sum(total[0:1, :], axis=1, keepdims=True)
    square = jnp.sum(total[1:2, :], axis=1, keepdims=True)
    return along, square


def step_of(count, along, square):
    theta = along / (square + EPS)
    scale = 1.0 / jnp.sqrt(square / count + EPS)

    def step(vector, hv, dh):
        resid = hv - theta * vector
        return (vector - STEP_SIZE * resid / (1.0 + jnp.abs(dh - theta))) * scale

    return theta, step


def iter_kernel(count, partners, ranks_ref, buf, vec_in, image_in, dh, *refs):
    parts = refs[:partners]
    vec, image, part = refs[partners:]
    _, step = step_of(count, *joined(parts))
    apply_all(lambda s: step(vec_in[s], image_in[s], dh[s]), ranks_ref, buf, vec, image, part)


def last_kernel(count, partners, vec_in, image_in, dh, *refs):
    parts = refs[:partners]
    vec, part, energy = refs[partners:]
    theta, step = step_of(count, *joined(parts))
    square = jnp.zeros(dh.shape[1:], F32)
    for s in range(dh.shape[0]):
        vector = step(vec_in[s], image_in[s], dh[s])
        vec[s] = vector
        square = square + vector * vector
    store_sums(part, square, square)
    energy[...] = jnp.broadcast_to(theta, energy.shape)


def psi_kernel(count, partners, vec, *refs):
    parts = refs[:partners]
    psi = refs[partners]
    square, _ = joined(parts)
    scale = 1.0 / jnp.sqrt(square / count + EPS)
    for s in range(psi.shape[0]):
        psi[s] = (vec[s] * scale).astype(BF16)


def swap(value):
    size = lax.axis_size("chain")
    return lax.ppermute(value, "chain", [(c, c ^ 1) for c in range(size)])


def gather_parts(part):
    size = lax.axis_size("tensor")
    moved = [part]
    for m in range(1, size):
        moved.append(lax.ppermute(part, "tensor", [(t, t ^ m) for t in range(size)]))
    return moved


def local(env, site, seg_weight, ranks, mpo_mask):
    sectors, chans, edge = env.shape[1:4]
    blocks = sectors * chans
    pairs = (blocks + 1) // 2
    tensor = lax.axis_size("tensor")
    count = float(sectors * tensor * edge * edge)
    base = min(pairs, -(-pairs * 3 // 5))
    cuts = [(0, base // 2), (base // 2, base), (base, pairs)]
    rows = lambda cut: (cut[1] - cut[0]) * edge + -(-(cut[1] - cut[0]) // 16) * 16

    weights = lax.all_gather(seg_weight[0], "chain")
    other_site = swap(site[0])
    block_bytes = 2 * edge * edge
    big = sectors * edge * edge * 4
    flat_env = env.reshape(blocks, edge, edge)

    packed = pl.pallas_call(
        functools.partial(pack_kernel, cuts, sectors, chans),
        out_shape=[jax.ShapeDtypeStruct((rows(c), edge), BF16) for c in cuts]
        + [jax.ShapeDtypeStruct((4, blocks + 8), jnp.int32)],
        in_specs=[SM, VM],
        out_specs=[VM] * len(cuts) + [SM],
        scratch_shapes=[pltpu.VMEM((max(-(-(c[1] - c[0]) // 16) * 16 for c in cuts), edge), F32)],
        compiler_params=params(),
        cost_estimate=cost(0, 2 * blocks * block_bytes),
        name="pack",
    )(mpo_mask, flat_env)
    sent, where = packed[:-1], packed[-1]
    got = [swap(c) for c in sent[:2]]
    active = jnp.sum(mpo_mask)
    got.append(lax.cond(active > 2 * base, swap, lambda c: c, sent[2]))

    buf_shape = (2, sectors, chans, edge, edge)
    diag_shape = (2, sectors, -(-chans // 16) * 16, edge)
    outer_shape = (sectors, edge, edge)
    buf, diags, outer = pl.pallas_call(
        functools.partial(own_kernel, cuts[0]),
        out_shape=[vmem(buf_shape, BF16), vmem(diag_shape, F32), vmem(outer_shape, F32)],
        in_specs=[SM, VM, VM, VM],
        out_specs=[VM] * 3,
        scratch_shapes=[pltpu.VMEM(outer_shape, F32)],
        compiler_params=params(),
        cost_estimate=cost(0, 4 * blocks * block_bytes),
        name="own",
    )(where, flat_env, weights, got[0])

    state = vmem(outer_shape, F32)
    sums = jax.ShapeDtypeStruct((2, edge), F32)
    work = 4.0 * blocks * edge**3
    buf, diags, vec, image, dh, part = pl.pallas_call(
        functools.partial(first_kernel, cuts[1:]),
        out_shape=[vmem(buf_shape, BF16), vmem(diag_shape, F32), state, state, state, sums],
        in_specs=[SM, SM] + [VM] * 7,
        out_specs=[VM] * 6,
        input_output_aliases={7: 0, 8: 1},
        compiler_params=params(),
        cost_estimate=cost(work, 2 * blocks * block_bytes),
        name="first",
    )(where, ranks, keep(outer), site[0], other_site, got[1], got[2], keep(buf), keep(diags))

    for _ in range(ITERS - 1):
        parts = gather_parts(part)
        vec, image, part = pl.pallas_call(
            functools.partial(iter_kernel, count, tensor),
            out_shape=[state, state, sums],
            in_specs=[SM] + [VM] * (4 + tensor),
            out_specs=[VM] * 3,
            compiler_params=params(),
            cost_estimate=cost(work, 2 * blocks * block_bytes),
            name="iterate",
        )(ranks, keep(buf), keep(vec), keep(image), keep(dh), *parts)

    parts = gather_parts(part)
    vec, part, energy = pl.pallas_call(
        functools.partial(last_kernel, count, tensor),
        out_shape=[state, sums, jax.ShapeDtypeStruct((1, edge), F32)],
        in_specs=[VM] * (3 + tensor),
        out_specs=[VM] * 3,
        compiler_params=params(),
        cost_estimate=cost(0, 3 * big),
        name="last",
    )(keep(vec), keep(image), keep(dh), *parts)
    parts = gather_parts(part)
    psi = pl.pallas_call(
        functools.partial(psi_kernel, count, tensor),
        out_shape=jax.ShapeDtypeStruct(outer_shape, BF16),
        in_specs=[VM] * (1 + tensor),
        out_specs=VM,
        compiler_params=params(),
        cost_estimate=cost(0, big),
        name="psi",
    )(keep(vec), *parts)
    return psi[None], energy[0, :1]


def solution(mesh):
    in_specs = (
        P(("cyl", "chain"), "tensor", None, None, None),
        P(("cyl", "chain"), "tensor", None, None),
        P(("cyl", "chain"), "tensor", None),
        P(("cyl", "tensor")),
        P(("cyl", "tensor"), None),
    )
    out_specs = (P(("cyl", "chain"), "tensor", None, None), P(("cyl", "chain")))
    return jax.shard_map(local, mesh=mesh, in_specs=in_specs, out_specs=out_specs, check_vma=False)
```

time: 209 us -> 97 us (0.46)
  waiting for transfers between devices: 59.2 us -> 10.4 us
  local copies, waits for them, and re-layouts: 53.1 us -> 6.31 us
  Pallas kernels: 0 us -> 33.1 us
  matrix products: 23.5 us -> 0 us
  blocking collectives: 45.4 us -> 28.7 us
  starting transfers between devices: 2.09 us -> 15.7 us
  other arithmetic: 13.5 us -> 1.32 us
  between operations: 10.6 us -> 1.41 us
    ppermute x2 -> x18, waiting for transfers between devices: 59.2 us -> 10.4 us  [the longest x15 10.4 us: gather_parts(): lax.ppermute(part, 'tensor', [(t, t ^ m) for t in range(size)])]
    cond x7 -> x0, local copies, waits for them, and re-layouts: 44.8 us -> none  [the longest x2 39.9 us: order_roles(): lax.cond(is_left, lambda: (own_env, other_env, own_site, other_site), lam...]
    pallas_call x0 -> x8, Pallas kernels: none -> 33.1 us  [the longest x3 15.4 us: local(): pl.pallas_call(functools.partial(iter_kernel, count, tensor), out_shape=[...]
    psum x5 -> x0, blocking collectives: 30.5 us -> none  [totals(): return lax.psum(values, 'tensor')]
    dot_general x10 -> x0, matrix products: 23.5 us -> none  [the longest x4 16.2 us: solve_boundary(): jnp.einsum('sxi,sxk->sik', left_flat, inner_flat, preferred_element_type=...]
    all_gather x1, blocking collectives: 14.9 us -> 28.7 us  [local(): weights = lax.all_gather(seg_weight[0], 'chain')]
    ppermute x2 -> x18, starting transfers between devices: 2.09 us -> 15.7 us  [the longest x15 10.6 us: gather_parts(): lax.ppermute(part, 'tensor', [(t, t ^ m) for t in range(size)])]
    another operation x4 -> x0, other arithmetic: 5.46 us -> none  [solve_boundary(): jnp.stack([jnp.sum(vector * image), jnp.sum(vector * vector)])]
  transfers between devices with their start and end apart: 2 -> 18, of which waited for: 1 -> 10; matrix products, arithmetic and copies ran while one was open for 0% -> 1% of each run, Pallas kernels for 0% -> 7%
where the time goes in v1:
time: 97 us
  Pallas kernels  33.1 us (34%)
  blocking collectives  28.7 us (30%)
  starting transfers between devices  15.7 us (16%)
  waiting for transfers between devices  10.4 us (11%)
  local copies, waits for them, and re-layouts  6.31 us (7%)
  between operations  1.41 us (1%)
  other arithmetic  1.32 us (1%)
    all_gather x1, blocking collectives, local(): weights = lax.all_gather(seg_weight[0], 'chain')  28.7 us
    pallas_call x3, Pallas kernels, local(): pl.pallas_call(functools.partial(iter_kernel, count, tensor), out_shape=[...  15.4 us
    ppermute x15, starting transfers between devices, gather_parts(): lax.ppermute(part, 'tensor', [(t, t ^ m) for t in range(size)])  10.6 us
    ppermute x15, waiting for transfers between devices, gather_parts(): lax.ppermute(part, 'tensor', [(t, t ^ m) for t in range(size)])  10.4 us
    pallas_call x1, Pallas kernels, local(): pl.pallas_call(functools.partial(first_kernel, cuts[1:]), out_shape=[vmem...  7.4 us
    pallas_call x1, Pallas kernels, local(): pl.pallas_call(functools.partial(own_kernel, cuts[0]), out_shape=[vmem(bu...  6.72 us
    unnamed x32, local copies, waits for them, and re-layouts  6.31 us
    ppermute x3, starting transfers between devices, swap(): return lax.ppermute(value, 'chain', [(c, c ^ 1) for c in range(size)])  5.11 us
  transfers between devices with their start and end apart: 18, of which 10 were waited for; matrix products, arithmetic and copies ran while one was open for 1% of the time, Pallas kernels for 7%

profile of v1, /device:TPU:0, one launch (start us, length us, event | category | flops | bytes accessed | tf_op | source)
XLA Modules:
  0.0 97.0 jit_solution(11900380884958651406)
XLA Ops:
  0.6 0.0 copy-start
  0.6 1.7 %copy-done = bf16[1,8,10,128,128]{4,3,2,1,0:T(8,128)(2,1)S(1)} copy-done((bf16[1,8,10,128,128]{4,3,2,1,0:T(8,128)(2,1)S(1)}, bf16[1,8,10,128,128]{4,3,2,1,0:T(8,128)(2,1)}, u32[]{:S(2)}) %copy-start) | copy-done | bytes 2621464
  2.4 0.7 copy-done.1
  3.1 2.1 %pack.1 = (bf16[1552,128]{1,0:T(8,128)(2,1)S(1)}, bf16[1552,128]{1,0:T(8,128)(2,1)S(1)}, bf16[2064,128]{1,0:T(8,128)(2,1)S(1)}, s32[4,88]{1,0:T(4,128)S(1)}) custom-call(s32[8,10]{1,0:T(8,128)S(1)} %copy-done.1, bf16[80,128,128]{2,1,0:T(8,128)(2,1)S(1)} %bitcast.6), custom_call_target="tpu_custom_call" | custom-call | bytes 5242880 | tf_op jit(solution)/shard_map/pack/pallas_call | solution.py:289
  5.1 0.0 copy-start.2
  5.2 3.1 %collective-permute-start.1 = (bf16[1552,128]{1,0:T(8,128)(2,1)S(1)}, bf16[1552,128]{1,0:T(8,128)(2,1)S(1)}, u32[]{:S(2)}, u32[]{:S(2)}) collective-permute-start(bf16[1552,128]{1,0:T(8,128)(2,1)S(1)} %get-tuple-element.32), channel_id=1, source_target_pairs={{0,4},{4,0},{8,12},{12,8},{1,5},{5,1},{9,13},{13,9},{2,6},{6,2},{1... | collective-permute-start | bytes 1191944 | tf_op jit(solution)/shard_map/ppermute | solution.py:262
  8.2 0.1 collective-permute-start.3
  8.3 1.9 %collective-permute-start.2 = (bf16[8,128,128]{2,1,0:T(8,128)(2,1)}, bf16[8,128,128]{2,1,0:T(8,128)(2,1)S(1)}, u32[]{:S(2)}, u32[]{:S(2)}) collective-permute-start(bf16[8,128,128]{2,1,0:T(8,128)(2,1)} %bitcast.7), channel_id=1, source_target_pairs={{0,4},{4,0},{8,12},{12,8},{1,5},{5,1},{9,13},{13,9},{2,6},{6,2},{1... | collective-permute-start | bytes 786440 | tf_op jit(solution)/shard_map/ppermute | solution.py:262
  10.3 1.3 %reduce_sum.9 = s32[]{:T(128)} reduce(s32[8,10]{1,0:T(8,128)} %mask_ref.1, s32[]{:T(128)} %constant.0.clone.1), dimensions={0,1}, to_apply=%region_0.0 | reduce | flops 79 | bytes 328 | tf_op jit(solution)/shard_map/reduce_sum | solution.py:302
  12.3 28.7 %all_gather.3.weights = f32[4,8,128]{2,1,0:T(8,128)S(1)} all-gather(f32[1,8,128]{2,1,0:T(8,128)} %param.9), channel_id=1, replica_groups=mesh['cyl'=2,'chain'=4,'tensor'=4] {'chain'}, dimensions={0}, use_global_device_ids=true | all-gather | bytes 20480 | tf_op jit(solution)/shard_map/all_gather | solution.py:283
  41.0 0.0 collective-permute-done.1.chunk
  41.0 0.8 copy-done.5
  41.7 6.7 %own.1 = (bf16[2,8,10,128,128]{4,3,2,1,0:T(8,128)(2,1)S(1)}, f32[2,8,16,128]{3,2,1,0:T(8,128)S(1)}, f32[8,128,128]{2,1,0:T(8,128)S(1)}) custom-call(s32[4,88]{1,0:T(4,128)S(1)} %get-tuple-element.31.where_ref, bf16[80,128,128]{2,1,0:T(8,128)(2,1)} %bitcast.5, f32[4,8,128]{2,1,0:T(8,128)S(1)} %all_gather.3.weights, bf16[1552,128]{1,0:T(8,128)(2,1)} %copy-done.5), custom_call_target="tpu_custom_call" | custom-call | bytes 10485760 | tf_op jit(solution)/shard_map/own/pallas_call | solution.py:308
  48.4 0.0 collective-permute-done.2.other_site
  48.5 0.0 copy-start.6
  48.5 0.0 collective-permute-done.3.refs_0_
  48.5 0.0 copy-start.4
  48.5 0.0 copy-done.2
  48.5 0.7 copy-done.6
  49.2 0.1 copy-done.4
  49.3 7.4 %first.1 = (bf16[2,8,10,128,128]{4,3,2,1,0:T(8,128)(2,1)S(1)}, f32[2,8,16,128]{3,2,1,0:T(8,128)S(1)}, f32[8,128,128]{2,1,0:T(8,128)S(1)}, f32[8,128,128]{2,1,0:T...) custom-call(s32[4,88]{1,0:T(4,128)} %copy-done.2, ...), custom_call_target="tpu_custom_call", output_to_operand_aliasing={{0}: (7, {}), {1}: (8, {})} | custom-call | flops 671088640 | bytes 5242880 | tf_op jit(solution)/shard_map/first/pallas_call | solution.py:322
  56.7 0.0 collective-permute-start.6
  56.7 2.3 %collective-permute-start.5 = (f32[2,128]{1,0:T(2,128)}, f32[2,128]{1,0:T(2,128)S(1)}, u32[]{:S(2)}, u32[]{:S(2)}) collective-permute-start(f32[2,128]{1,0:T(2,128)} %get-tuple-element.42.refs_0_), channel_id=1, source_target_pairs={{0,2},{1,3},{2,0},{3,1},{4,6},{5,7},{6,4},{7,5},{8,10},{9,11},{10,... | collective-permute-start | bytes 3080 | tf_op jit(solution)/shard_map/ppermute | solution.py:269
  59.0 0.1 collective-permute-start.4
  59.1 0.8 collective-permute-done.6.refs_3_
  59.9 0.8 collective-permute-done.5.refs_2_
  60.7 0.0 collective-permute-done.4.refs_1_
  60.8 0.0 copy-done.8
  60.8 0.5 copy-done.11
  61.3 0.0 copy-done.14
  61.3 5.1 %iterate.3 = (f32[8,128,128]{2,1,0:T(8,128)S(1)}, f32[8,128,128]{2,1,0:T(8,128)S(1)}, f32[2,128]{1,0:T(2,128)}) custom-call(s32[8]{0:T(128)} %ranks_ref.7, bf16[2,8,10,128,128]{4,3,2,1,0:T(8,128)(2,1)S(1)} %get-tuple-element.38.buf, f32[8,128,128]{2,1,0:T(8,128)S(1)} %get-tuple-element.39.vec_in, f32[8,128,128]{2,1,0:T(8,128)S(1)} %get-tuple-element.40.image_in, ...), custom_call_target="tpu_custom_call" | custom-call | flops 671088640 | bytes 5242880 | tf_op jit(solution)/shard_map/iterate/pallas_call | solution.py:335
  66.5 1.1 %collective-permute-start.9 = (f32[2,128]{1,0:T(2,128)}, f32[2,128]{1,0:T(2,128)S(1)}, u32[]{:S(2)}, u32[]{:S(2)}) collective-permute-start(f32[2,128]{1,0:T(2,128)} %get-tuple-element.45.refs_0_), channel_id=1, source_target_pairs={{0,3},{1,2},{2,1},{3,0},{4,7},{5,6},{6,5},{7,4},{8,11},{9,10},{10,... | collective-permute-start | bytes 3080 | tf_op jit(solution)/shard_map/ppermute | solution.py:269
  67.6 1.5 %collective-permute-start.8 = (f32[2,128]{1,0:T(2,128)}, f32[2,128]{1,0:T(2,128)S(1)}, u32[]{:S(2)}, u32[]{:S(2)}) collective-permute-start(f32[2,128]{1,0:T(2,128)} %get-tuple-element.45.refs_0_), channel_id=1, source_target_pairs={{0,2},{1,3},{2,0},{3,1},{4,6},{5,7},{6,4},{7,5},{8,10},{9,11},{10,... | collective-permute-start | bytes 3080 | tf_op jit(solution)/shard_map/ppermute | solution.py:269
  69.0 0.0 collective-permute-start.7
  69.0 0.6 collective-permute-done.9.refs_3_
  69.7 1.7 %collective-permute-done.8.refs_2_ = f32[2,128]{1,0:T(2,128)S(1)} collective-permute-done((f32[2,128]{1,0:T(2,128)}, f32[2,128]{1,0:T(2,128)S(1)}, u32[]{:S(2)}, u32[]{:S(2)}) %collective-permute-start.8) | collective-permute-done | bytes 1056 | tf_op jit(solution)/shard_map/ppermute | solution.py:269
  71.4 0.0 collective-permute-done.7.refs_1_
  71.4 0.5 copy-done.12
  71.9 0.0 copy-done.15
  71.9 5.1 %iterate.4 = (f32[8,128,128]{2,1,0:T(8,128)S(1)}, f32[8,128,128]{2,1,0:T(8,128)S(1)}, f32[2,128]{1,0:T(2,128)}) custom-call(s32[8]{0:T(128)} %ranks_ref.7, bf16[2,8,10,128,128]{4,3,2,1,0:T(8,128)(2,1)S(1)} %get-tuple-element.38.buf, f32[8,128,128]{2,1,0:T(8,128)S(1)} %get-tuple-element.43.vec_in, f32[8,128,128]{2,1,0:T(8,128)S(1)} %get-tuple-element.44.image_in, ...), custom_call_target="tpu_custom_call" | custom-call | flops 671088640 | bytes 5242880 | tf_op jit(solution)/shard_map/iterate/pallas_call | solution.py:335
  77.0 0.0 collective-permute-start.12
  77.1 1.7 %collective-permute-start.11 = (f32[2,128]{1,0:T(2,128)}, f32[2,128]{1,0:T(2,128)S(1)}, u32[]{:S(2)}, u32[]{:S(2)}) collective-permute-start(f32[2,128]{1,0:T(2,128)} %get-tuple-element.48.refs_0_), channel_id=1, source_target_pairs={{0,2},{1,3},{2,0},{3,1},{4,6},{5,7},{6,4},{7,5},{8,10},{9,11},{10,... | collective-permute-start | bytes 3080 | tf_op jit(solution)/shard_map/ppermute | solution.py:269
  78.8 0.1 collective-permute-start.10
  78.9 1.2 %collective-permute-done.12.refs_3_ = f32[2,128]{1,0:T(2,128)S(1)} collective-permute-done((f32[2,128]{1,0:T(2,128)}, f32[2,128]{1,0:T(2,128)S(1)}, u32[]{:S(2)}, u32[]{:S(2)}) %collective-permute-start.12) | collective-permute-done | bytes 1056 | tf_op jit(solution)/shard_map/ppermute | solution.py:269
  80.1 0.8 collective-permute-done.11.refs_2_
  80.9 0.0 collective-permute-done.10.refs_1_
  80.9 0.6 copy-done.10
  81.4 0.0 copy-done.13
  81.4 5.1 %iterate.5 = (f32[8,128,128]{2,1,0:T(8,128)S(1)}, f32[8,128,128]{2,1,0:T(8,128)S(1)}, f32[2,128]{1,0:T(2,128)}) custom-call(s32[8]{0:T(128)} %ranks_ref.7, bf16[2,8,10,128,128]{4,3,2,1,0:T(8,128)(2,1)S(1)} %get-tuple-element.38.buf, f32[8,128,128]{2,1,0:T(8,128)S(1)} %get-tuple-element.46.vec_in, f32[8,128,128]{2,1,0:T(8,128)S(1)} %get-tuple-element.47.image_in, ...), custom_call_target="tpu_custom_call" | custom-call | flops 671088640 | bytes 5242880 | tf_op jit(solution)/shard_map/iterate/pallas_call | solution.py:335
  86.6 0.4 collective-permute-start.15
  87.0 1.4 %collective-permute-start.14 = (f32[2,128]{1,0:T(2,128)}, f32[2,128]{1,0:T(2,128)S(1)}, u32[]{:S(2)}, u32[]{:S(2)}) collective-permute-start(f32[2,128]{1,0:T(2,128)} %get-tuple-element.51.refs_0_), channel_id=1, source_target_pairs={{0,2},{1,3},{2,0},{3,1},{4,6},{5,7},{6,4},{7,5},{8,10},{9,11},{10,... | collective-permute-start | bytes 3080 | tf_op jit(solution)/shard_map/ppermute | solution.py:269
  88.4 0.0 collective-permute-start.13
  88.4 1.3 %collective-permute-done.15.refs_3_ = f32[2,128]{1,0:T(2,128)S(1)} collective-permute-done((f32[2,128]{1,0:T(2,128)}, f32[2,128]{1,0:T(2,128)S(1)}, u32[]{:S(2)}, u32[]{:S(2)}) %collective-permute-start.15) | collective-permute-done | bytes 1056 | tf_op jit(solution)/shard_map/ppermute | solution.py:269
  89.8 1.0 %collective-permute-done.14.refs_2_ = f32[2,128]{1,0:T(2,128)S(1)} collective-permute-done((f32[2,128]{1,0:T(2,128)}, f32[2,128]{1,0:T(2,128)S(1)}, u32[]{:S(2)}, u32[]{:S(2)}) %collective-permute-start.14) | collective-permute-done | bytes 1056 | tf_op jit(solution)/shard_map/ppermute | solution.py:269
  90.8 0.0 collective-permute-done.13.refs_1_
  90.8 0.6 copy-done.3
  91.4 0.7 last.1
  92.1 0.4 collective-permute-start.18
  92.5 1.5 %collective-permute-start.17 = (f32[2,128]{1,0:T(2,128)S(1)}, f32[2,128]{1,0:T(2,128)S(1)}, u32[]{:S(2)}, u32[]{:S(2)}) collective-permute-start(f32[2,128]{1,0:T(2,128)S(1)} %get-tuple-element.53.refs_0_), channel_id=1, source_target_pairs={{0,2},{1,3},{2,0},{3,1},{4,6},{5,7},{6,4},{7,5},{8,10},{9,11},{10,... | collective-permute-start | bytes 3080 | tf_op jit(solution)/shard_map/ppermute | solution.py:269
  94.0 0.0 collective-permute-start.16
  94.0 1.1 %collective-permute-done.18.refs_3_ = f32[2,128]{1,0:T(2,128)S(1)} collective-permute-done((f32[2,128]{1,0:T(2,128)S(1)}, f32[2,128]{1,0:T(2,128)S(1)}, u32[]{:S(2)}, u32[]{:S(2)}) %collective-permute-start.18) | collective-permute-done | bytes 1056 | tf_op jit(solution)/shard_map/ppermute | solution.py:269
  95.1 1.0 %collective-permute-done.17.refs_2_ = f32[2,128]{1,0:T(2,128)S(1)} collective-permute-done((f32[2,128]{1,0:T(2,128)S(1)}, f32[2,128]{1,0:T(2,128)S(1)}, u32[]{:S(2)}, u32[]{:S(2)}) %collective-permute-start.17) | collective-permute-done | bytes 1056 | tf_op jit(solution)/shard_map/ppermute | solution.py:269
  96.1 0.0 collective-permute-done.16.refs_1_
  96.1 0.8 psi.1
  (15 shorter events, 0.0 us)
Async XLA Ops:
  0.6 1.7 %copy-start = (bf16[1,8,10,128,128]{4,3,2,1,0:T(8,128)(2,1)S(1)}, bf16[1,8,10,128,128]{4,3,2,1,0:T(8,128)(2,1)}, u32[]{:S(2)}) copy-start(bf16[1,8,10,128,128]{4,3,2,1,0:T(8,128)(2,1)} %param.7) | copy-start | bytes 7864324
  2.4 0.7 copy-start.1
  5.1 43.3 %copy-start.2 = (s32[4,88]{1,0:T(4,128)}, s32[4,88]{1,0:T(4,128)S(1)}, u32[]{:S(2)}) copy-start(s32[4,88]{1,0:T(4,128)S(1)} %get-tuple-element.31.where_ref) | copy-start | bytes 4228
  5.2 35.8 %collective-permute-start.1 = (bf16[1552,128]{1,0:T(8,128)(2,1)S(1)}, bf16[1552,128]{1,0:T(8,128)(2,1)S(1)}, u32[]{:S(2)}, u32[]{:S(2)}) collective-permute-start(bf16[1552,128]{1,0:T(8,128)(2,1)S(1)} %get-tuple-element.32), channel_id=1, source_target_pairs={{0,4},{4,0},{8,12},{12,8},{1,5},{5,1},{9,13},{13,9},{2,6},{6,2},{1... | collective-permute-start | bytes 1191944 | tf_op jit(solution)/shard_map/ppermute | solution.py:262
  8.2 40.2 %collective-permute-start.3 = (bf16[1552,128]{1,0:T(8,128)(2,1)S(1)}, bf16[1552,128]{1,0:T(8,128)(2,1)S(1)}, u32[]{:S(2)}, u32[]{:S(2)}) collective-permute-start(bf16[1552,128]{1,0:T(8,128)(2,1)S(1)} %get-tuple-element.34), channel_id=1, source_target_pairs={{0,4},{4,0},{8,12},{12,8},{1,5},{5,1},{9,13},{13,9},{2,6},{6,2},{1... | collective-permute-start | bytes 1191944 | tf_op jit(solution)/shard_map/ppermute | solution.py:262
  8.3 40.1 %collective-permute-start.2 = (bf16[8,128,128]{2,1,0:T(8,128)(2,1)}, bf16[8,128,128]{2,1,0:T(8,128)(2,1)S(1)}, u32[]{:S(2)}, u32[]{:S(2)}) collective-permute-start(bf16[8,128,128]{2,1,0:T(8,128)(2,1)} %bitcast.7), channel_id=1, source_target_pairs={{0,4},{4,0},{8,12},{12,8},{1,5},{5,1},{9,13},{13,9},{2,6},{6,2},{1... | collective-permute-start | bytes 786440 | tf_op jit(solution)/shard_map/ppermute | solution.py:262
  41.0 0.8 copy-start.5
  48.5 0.7 copy-start.6
  48.5 0.8 copy-start.4
  56.7 3.2 %collective-permute-start.6 = (f32[2,128]{1,0:T(2,128)}, f32[2,128]{1,0:T(2,128)S(1)}, u32[]{:S(2)}, u32[]{:S(2)}) collective-permute-start(f32[2,128]{1,0:T(2,128)} %get-tuple-element.42.refs_0_), channel_id=1, source_target_pairs={{0,3},{1,2},{2,1},{3,0},{4,7},{5,6},{6,5},{7,4},{8,11},{9,10},{10,... | collective-permute-start | bytes 3080 | tf_op jit(solution)/shard_map/ppermute | solution.py:269
  56.7 4.1 %collective-permute-start.5 = (f32[2,128]{1,0:T(2,128)}, f32[2,128]{1,0:T(2,128)S(1)}, u32[]{:S(2)}, u32[]{:S(2)}) collective-permute-start(f32[2,128]{1,0:T(2,128)} %get-tuple-element.42.refs_0_), channel_id=1, source_target_pairs={{0,2},{1,3},{2,0},{3,1},{4,6},{5,7},{6,4},{7,5},{8,10},{9,11},{10,... | collective-permute-start | bytes 3080 | tf_op jit(solution)/shard_map/ppermute | solution.py:269
  59.0 1.8 %collective-permute-start.4 = (f32[2,128]{1,0:T(2,128)}, f32[2,128]{1,0:T(2,128)S(1)}, u32[]{:S(2)}, u32[]{:S(2)}) collective-permute-start(f32[2,128]{1,0:T(2,128)} %get-tuple-element.42.refs_0_), channel_id=1, source_target_pairs={{0,1},{1,0},{2,3},{3,2},{4,5},{5,4},{6,7},{7,6},{8,9},{9,8},{10,11... | collective-permute-start | bytes 3080 | tf_op jit(solution)/shard_map/ppermute | solution.py:269
  59.9 0.9 copy-start.8
  60.7 0.5 copy-start.11
  60.7 0.6 copy-start.14
  66.5 3.2 %collective-permute-start.9 = (f32[2,128]{1,0:T(2,128)}, f32[2,128]{1,0:T(2,128)S(1)}, u32[]{:S(2)}, u32[]{:S(2)}) collective-permute-start(f32[2,128]{1,0:T(2,128)} %get-tuple-element.45.refs_0_), channel_id=1, source_target_pairs={{0,3},{1,2},{2,1},{3,0},{4,7},{5,6},{6,5},{7,4},{8,11},{9,10},{10,... | collective-permute-start | bytes 3080 | tf_op jit(solution)/shard_map/ppermute | solution.py:269
  67.6 3.8 %collective-permute-start.8 = (f32[2,128]{1,0:T(2,128)}, f32[2,128]{1,0:T(2,128)S(1)}, u32[]{:S(2)}, u32[]{:S(2)}) collective-permute-start(f32[2,128]{1,0:T(2,128)} %get-tuple-element.45.refs_0_), channel_id=1, source_target_pairs={{0,2},{1,3},{2,0},{3,1},{4,6},{5,7},{6,4},{7,5},{8,10},{9,11},{10,... | collective-permute-start | bytes 3080 | tf_op jit(solution)/shard_map/ppermute | solution.py:269
  69.0 2.3 %collective-permute-start.7 = (f32[2,128]{1,0:T(2,128)}, f32[2,128]{1,0:T(2,128)S(1)}, u32[]{:S(2)}, u32[]{:S(2)}) collective-permute-start(f32[2,128]{1,0:T(2,128)} %get-tuple-element.45.refs_0_), channel_id=1, source_target_pairs={{0,1},{1,0},{2,3},{3,2},{4,5},{5,4},{6,7},{7,6},{8,9},{9,8},{10,11... | collective-permute-start | bytes 3080 | tf_op jit(solution)/shard_map/ppermute | solution.py:269
  69.7 1.7 %copy-start.9 = (f32[2,128]{1,0:T(2,128)}, f32[2,128]{1,0:T(2,128)S(1)}, u32[]{:S(2)}) copy-start(f32[2,128]{1,0:T(2,128)S(1)} %collective-permute-done.9.refs_3_) | copy-start | bytes 3076
  71.4 0.5 copy-start.12
  71.4 0.6 copy-start.15
  77.0 3.1 %collective-permute-start.12 = (f32[2,128]{1,0:T(2,128)}, f32[2,128]{1,0:T(2,128)S(1)}, u32[]{:S(2)}, u32[]{:S(2)}) collective-permute-start(f32[2,128]{1,0:T(2,128)} %get-tuple-element.48.refs_0_), channel_id=1, source_target_pairs={{0,3},{1,2},{2,1},{3,0},{4,7},{5,6},{6,5},{7,4},{8,11},{9,10},{10,... | collective-permute-start | bytes 3080 | tf_op jit(solution)/shard_map/ppermute | solution.py:269
  77.1 3.8 %collective-permute-start.11 = (f32[2,128]{1,0:T(2,128)}, f32[2,128]{1,0:T(2,128)S(1)}, u32[]{:S(2)}, u32[]{:S(2)}) collective-permute-start(f32[2,128]{1,0:T(2,128)} %get-tuple-element.48.refs_0_), channel_id=1, source_target_pairs={{0,2},{1,3},{2,0},{3,1},{4,6},{5,7},{6,4},{7,5},{8,10},{9,11},{10,... | collective-permute-start | bytes 3080 | tf_op jit(solution)/shard_map/ppermute | solution.py:269
  78.8 2.1 %collective-permute-start.10 = (f32[2,128]{1,0:T(2,128)}, f32[2,128]{1,0:T(2,128)S(1)}, u32[]{:S(2)}, u32[]{:S(2)}) collective-permute-start(f32[2,128]{1,0:T(2,128)} %get-tuple-element.48.refs_0_), channel_id=1, source_target_pairs={{0,1},{1,0},{2,3},{3,2},{4,5},{5,4},{6,7},{7,6},{8,9},{9,8},{10,11... | collective-permute-start | bytes 3080 | tf_op jit(solution)/shard_map/ppermute | solution.py:269
  80.1 0.8 copy-start.7
  80.9 0.6 copy-start.10
  80.9 0.6 copy-start.13
  86.6 3.2 %collective-permute-start.15 = (f32[2,128]{1,0:T(2,128)}, f32[2,128]{1,0:T(2,128)S(1)}, u32[]{:S(2)}, u32[]{:S(2)}) collective-permute-start(f32[2,128]{1,0:T(2,128)} %get-tuple-element.51.refs_0_), channel_id=1, source_target_pairs={{0,3},{1,2},{2,1},{3,0},{4,7},{5,6},{6,5},{7,4},{8,11},{9,10},{10,... | collective-permute-start | bytes 3080 | tf_op jit(solution)/shard_map/ppermute | solution.py:269
  87.0 3.8 %collective-permute-start.14 = (f32[2,128]{1,0:T(2,128)}, f32[2,128]{1,0:T(2,128)S(1)}, u32[]{:S(2)}, u32[]{:S(2)}) collective-permute-start(f32[2,128]{1,0:T(2,128)} %get-tuple-element.51.refs_0_), channel_id=1, source_target_pairs={{0,2},{1,3},{2,0},{3,1},{4,6},{5,7},{6,4},{7,5},{8,10},{9,11},{10,... | collective-permute-start | bytes 3080 | tf_op jit(solution)/shard_map/ppermute | solution.py:269
  88.4 2.4 %collective-permute-start.13 = (f32[2,128]{1,0:T(2,128)}, f32[2,128]{1,0:T(2,128)S(1)}, u32[]{:S(2)}, u32[]{:S(2)}) collective-permute-start(f32[2,128]{1,0:T(2,128)} %get-tuple-element.51.refs_0_), channel_id=1, source_target_pairs={{0,1},{1,0},{2,3},{3,2},{4,5},{5,4},{6,7},{7,6},{8,9},{9,8},{10,11... | collective-permute-start | bytes 3080 | tf_op jit(solution)/shard_map/ppermute | solution.py:269
  90.8 0.6 copy-start.3
  92.1 3.0 %collective-permute-start.18 = (f32[2,128]{1,0:T(2,128)S(1)}, f32[2,128]{1,0:T(2,128)S(1)}, u32[]{:S(2)}, u32[]{:S(2)}) collective-permute-start(f32[2,128]{1,0:T(2,128)S(1)} %get-tuple-element.53.refs_0_), channel_id=1, source_target_pairs={{0,3},{1,2},{2,1},{3,0},{4,7},{5,6},{6,5},{7,4},{8,11},{9,10},{10,... | collective-permute-start | bytes 3080 | tf_op jit(solution)/shard_map/ppermute | solution.py:269
  92.5 3.6 %collective-permute-start.17 = (f32[2,128]{1,0:T(2,128)S(1)}, f32[2,128]{1,0:T(2,128)S(1)}, u32[]{:S(2)}, u32[]{:S(2)}) collective-permute-start(f32[2,128]{1,0:T(2,128)S(1)} %get-tuple-element.53.refs_0_), channel_id=1, source_target_pairs={{0,2},{1,3},{2,0},{3,1},{4,6},{5,7},{6,4},{7,5},{8,10},{9,11},{10,... | collective-permute-start | bytes 3080 | tf_op jit(solution)/shard_map/ppermute | solution.py:269
  94.0 2.1 %collective-permute-start.16 = (f32[2,128]{1,0:T(2,128)S(1)}, f32[2,128]{1,0:T(2,128)S(1)}, u32[]{:S(2)}, u32[]{:S(2)}) collective-permute-start(f32[2,128]{1,0:T(2,128)S(1)} %get-tuple-element.53.refs_0_), channel_id=1, source_target_pairs={{0,1},{1,0},{2,3},{3,2},{4,5},{5,4},{6,7},{7,6},{8,9},{9,8},{10,11... | collective-permute-start | bytes 3080 | tf_op jit(solution)/shard_map/ppermute | solution.py:269
